TPU v7x, 32 devices: a whole 2x2x4 slice. The times are simulated.
32 devices in a mesh: slab: 16 (over z, x, core), strip: 2 (over y).
Axes of the slice: x: 2, y: 2, z: 4, core: 2. Of those that a mesh axis runs over, the one named last changes fastest.
Arguments:
- query_rows: bfloat16 [128, 48, 4096], P('slab', 'strip'), may hold values from -8 to 8
- key_rows: bfloat16 [128, 48, 4096], P('slab', 'strip'), may hold values from -8 to 8
- value_rows: bfloat16 [128, 48, 4096], P('slab', 'strip'), may hold values from -6 to 6
- window_offsets: int32 [8, 3], replicated, may hold values from -1 to 1, as said below
Outputs:
- attended: bfloat16 [128, 48, 4096], P('slab', 'strip')
Inputs may be any that keep to these rules, and one draw needn't show every extreme that they name: `window_offsets`: each row is a tile offset (dt, dh, dw); the 8 rows are distinct, one of them is (0, 0, 0), some row has dt = -1 and some row has dt = 1.
All inputs are finite; a program needn't handle non-finite values.
Results may differ from a plain program's by a relative error of at most 0.0049.
Values may be sent and summed in bfloat16 or wider, within the bound.
A program may use at most 128 MiB of HBM per device.

v0:
```python
import jax
import jax.numpy as jnp
from jax import lax
from jax.sharding import PartitionSpec as P

HD = 128
TILE_T = 4
TILE_H = 8
TILE_W = 8


def swapped(value, axis, apart):
    mask = 2**apart
    pairs = [(source, source ^ mask) for source in range(lax.axis_size(axis))]
    return lax.ppermute(value, axis, pairs)


def from_behind(block, axis, distance):
    devices = range(lax.axis_size(axis))
    route = [(i - distance, i) for i in devices if i - distance in devices]
    return lax.ppermute(block, axis, route)


def pair_transpose(pieces, move_piece, bit_order):
    slab_pos = lax.axis_index("slab")
    shaped = pieces.reshape((2, 2, 2) + pieces.shape[1:])
    for bit_num in bit_order:
        axis_num = 2 - bit_num
        is_upper = slab_pos >> bit_num & 1 == 1
        lower_half = jnp.take(shaped, 0, axis=axis_num)
        upper_half = jnp.take(shaped, 1, axis=axis_num)
        kept_part = jnp.where(is_upper, upper_half, lower_half)
        sent_part = jnp.where(is_upper, lower_half, upper_half)
        got_part = move_piece(sent_part, bit_num)
        shaped = jnp.stack(
            [jnp.where(is_upper, got_part, kept_part), jnp.where(is_upper, kept_part, got_part)],
            axis=axis_num,
        )
    return shaped.reshape((8,) + shaped.shape[3:])


def widen_rims(own_cols, rim_cols, right_side):
    blank = jnp.zeros_like(rim_cols)
    return jnp.concatenate(
        [jnp.where(right_side, blank, rim_cols), own_cols, jnp.where(right_side, rim_cols, blank)],
        axis=-2,
    )


def send_tiles(segment, bit_num):
    return swapped(segment, "slab", bit_num)


def send_rows(segment, bit_num):
    return swapped(segment, "slab", bit_num)


def per_device(query_rows, key_rows, value_rows, window_offsets):
    bit_order = (0, 1, 2)
    line_count = query_rows.shape[0]
    stacked = jnp.stack([query_rows, key_rows, value_rows])
    by_head = lax.all_to_all(stacked, "strip", split_axis=3, concat_axis=2, tiled=True)
    full_width = by_head.shape[2]
    half_width = full_width // 2
    piece_width = by_head.shape[3] // 4
    device_heads = piece_width // HD
    pieces = by_head.reshape(3, line_count, 2, half_width, 4, piece_width).transpose(
        2, 4, 0, 1, 3, 5
    )
    pieces = pieces.reshape(8, 3, line_count, half_width, piece_width)
    arrived = pair_transpose(pieces, send_tiles, bit_order)
    tile_block = arrived.reshape(TILE_T, 2, 3, line_count, half_width, piece_width).transpose(
        2, 0, 1, 3, 4, 5
    )
    tile_block = tile_block.reshape(3, TILE_T, 2 * line_count, half_width, piece_width)
    query_block = tile_block[0]
    key_value = tile_block[1:]
    slab_pos = lax.axis_index("slab")
    frame_tile = slab_pos // 8
    side_half = slab_pos // 4 % 2
    right_side = side_half == 0
    edge_cols = jnp.where(
        right_side, key_value[..., half_width - TILE_W :, :], key_value[..., :TILE_W, :]
    )
    rim_cols = swapped(edge_cols, "slab", 2)
    carried = jnp.concatenate([key_value, rim_cols], axis=-2)
    earlier_layer = from_behind(carried, "slab", 8)
    later_layer = from_behind(carried, "slab", -8)
    extended = jnp.stack(
        [
            widen_rims(layer_data[..., :half_width, :], layer_data[..., half_width:, :], right_side)
            for layer_data in (earlier_layer, carried, later_layer)
        ]
    )
    tile_rows = 2 * line_count // TILE_H
    tile_cols = half_width // TILE_W
    wide_cols = tile_cols + 2
    tokens = TILE_T * TILE_H * TILE_W
    key_tiles = extended.reshape(
        3, 2, TILE_T, tile_rows, TILE_H, wide_cols, TILE_W, device_heads, HD
    )
    key_tiles = key_tiles.transpose(0, 3, 5, 1, 2, 4, 6, 7, 8).reshape(
        3 * tile_rows * wide_cols, 2, tokens, device_heads, HD
    )
    query_tiles = query_block.reshape(
        TILE_T, tile_rows, TILE_H, tile_cols, TILE_W, device_heads, HD
    )
    query_tiles = query_tiles.transpose(1, 3, 0, 2, 4, 5, 6).reshape(
        tile_rows * tile_cols, tokens, device_heads, HD
    )
    query_count = tile_rows * tile_cols
    window_count = window_offsets.shape[0]
    tile_ids = jnp.arange(query_count, dtype=jnp.int32)
    row_tile = (tile_ids // tile_cols)[:, None]
    col_local = (tile_ids % tile_cols)[:, None]
    shift_frame = window_offsets[:, 0][None, :]
    shift_row = window_offsets[:, 1][None, :]
    shift_col = window_offsets[:, 2][None, :]
    key_frame = frame_tile + shift_frame
    key_row = row_tile + shift_row
    key_col = side_half * tile_cols + col_local + shift_col
    frame_total = lax.axis_size("slab") // 8
    inside = (key_frame >= 0) & (key_frame < frame_total) & (key_row >= 0) & (key_row < tile_rows)
    inside = inside & (key_col >= 0) & (key_col < 2 * tile_cols)
    flat_index = (
        (1 + shift_frame) * (tile_rows * wide_cols)
        + jnp.clip(key_row, 0, tile_rows - 1) * wide_cols
        + 1
        + col_local
        + shift_col
    )
    tiles_step = min(query_count, max(1, 512 // tokens))
    step_count = query_count // tiles_step
    score_scale = HD ** (-0.5)

    def attend(inputs):
        query_tile, tile_index, tile_live = inputs
        window_tiles = jnp.take(key_tiles, tile_index.reshape(-1), axis=0)
        window_tiles = window_tiles.reshape(tiles_step, window_count, 2, tokens, device_heads, HD)
        window_keys = window_tiles[:, :, 0].reshape(
            tiles_step, window_count * tokens, device_heads, HD
        )
        window_values = window_tiles[:, :, 1].reshape(
            tiles_step, window_count * tokens, device_heads, HD
        )
        scores = jnp.einsum(
            "pqhd,pkhd->phqk", query_tile, window_keys, preferred_element_type=jnp.float32
        )
        key_live = jnp.repeat(tile_live, tokens, axis=1)
        scores = jnp.where(key_live[:, None, None, :], scores, -1e30)
        row_max = jnp.max(scores, axis=-1, keepdims=True)
        raised = jnp.exp((scores - row_max) * score_scale)
        weights = (raised / jnp.sum(raised, axis=-1, keepdims=True)).astype(jnp.bfloat16)
        mixed_out = jnp.einsum(
            "phqk,pkhd->pqhd", weights, window_values, preferred_element_type=jnp.float32
        )
        return mixed_out.astype(jnp.bfloat16)

    attended = lax.map(
        attend,
        (
            query_tiles.reshape(step_count, tiles_step, tokens, device_heads, HD),
            flat_index.reshape(step_count, tiles_step, window_count),
            inside.reshape(step_count, tiles_step, window_count),
        ),
    )
    attended = attended.reshape(tile_rows, tile_cols, TILE_T, TILE_H, TILE_W, device_heads, HD)
    attended = attended.transpose(2, 0, 3, 1, 4, 5, 6).reshape(
        8, line_count, half_width, piece_width
    )
    returned = pair_transpose(attended, send_rows, bit_order)
    merged = returned.reshape(2, 4, line_count, half_width, piece_width).transpose(2, 0, 3, 1, 4)
    merged = merged.reshape(line_count, full_width, 4 * piece_width)
    return lax.all_to_all(merged, "strip", split_axis=1, concat_axis=2, tiled=True)


def solution(mesh):
    return jax.shard_map(
        per_device,
        mesh=mesh,
        in_specs=(
            P("slab", "strip", None),
            P("slab", "strip", None),
            P("slab", "strip", None),
            P(),
        ),
        out_specs=P("slab", "strip", None),
        check_vma=False,
    )
```

profile of v0, /device:TPU:0, one launch (start us, length us, event | category | flops | bytes accessed | tf_op | source)
XLA Modules:
  0.0 810.6 jit_solution(14298881730732370991)
XLA Ops:
  5.1 23.2 %copy.87 = bf16[3,8,24,4096]{2,1,0,3:T(8,128)(2,1)} copy(bf16[3,8,24,4096]{3,2,1,0:T(8,128)(2,1)} %pad_maximum_fusion.3) | data formatting | bytes 9437184 | tf_op jit(solution)/shard_map/stack | solution.py:61
  28.3 45.4 %reshape.576 = bf16[2,2,589824]{2,1,0:T(2,128)(2,1)} reshape(bf16[4096,3,8,24]{3,2,1,0:T(8,128)(2,1)} %bitcast.238) | data formatting | bytes 9437184
  79.5 54.5 %all-to-all-done = bf16[2,2,589824]{2,1,0:T(2,128)(2,1)} async-done(((bf16[2,2,589824]{2,1,0:T(2,128)(2,1)}), bf16[2,2,589824]{2,1,0:T(2,128)(2,1)}, u32[]{:S(2)}, u32[]{:S(2)}) %all-to-all-start) | async-done | bytes 4718624 | tf_op jit(solution)/shard_map/all_to_all | solution.py:62
  134.1 49.0 %reshape.577 = bf16[4096,3,8,24]{3,2,1,0:T(8,128)(2,1)} reshape(bf16[2,2,589824]{2,1,0:T(2,128)(2,1)} %all-to-all-done) | data formatting | bytes 9437184
  183.1 25.3 %copy.88 = bf16[3,8,24,2,2048]{4,2,3,1,0:T(8,128)(2,1)} copy(bf16[3,8,24,2,2048]{2,1,0,4,3:T(8,128)(2,1)} %bitcast.239) | data formatting | bytes 9437184 | tf_op jit(solution)/shard_map/all_to_all | solution.py:62
  234.8 51.7 %collective-permute-done.1 = bf16[2,2,3,8,24,512]{5,4,3,2,0,1:T(8,128)(2,1)} collective-permute-done((bf16[2,2,3,8,24,512]{5,4,3,2,0,1:T(8,128)(2,1)S(1)}, bf16[2,2,3,8,24,512]{5,4,3,2,0,1:T(8,128)(2,1)}, u32[]{:S(2)}, u32[]{:S(2)}) %collective-permute-start.1) | collective-permute-done | bytes 2359328 | tf_op jit(solution)/shard_map/ppermute | solution.py:15
  294.8 51.0 %collective-permute-done.2 = bf16[2,2,3,8,24,512]{5,4,3,2,1,0:T(8,128)(2,1)} collective-permute-done((bf16[2,2,3,8,24,512]{5,4,3,2,1,0:T(8,128)(2,1)}, bf16[2,2,3,8,24,512]{5,4,3,2,1,0:T(8,128)(2,1)}, u32[]{:S(2)}, u32[]{:S(2)}) %collective-permute-start.2) | collective-permute-done | bytes 2359328 | tf_op jit(solution)/shard_map/ppermute | solution.py:15
  354.0 21.7 %collective-permute-done.3 = bf16[2,4,16,8,512]{4,3,2,1,0:T(8,128)(2,1)S(1)} collective-permute-done((bf16[2,4,16,8,512]{4,3,2,1,0:T(8,128)(2,1)S(1)}, bf16[2,4,16,8,512]{4,3,2,1,0:T(8,128)(2,1)S(1)}, u32[]{:S(2)}, u32[]{:S(2)}) %collective-permute-start.3) | collective-permute-done | bytes 1048608 | tf_op jit(solution)/shard_map/ppermute | solution.py:15
  390.5 80.4 %collective-permute-done.4 = bf16[2,4,16,32,512]{4,3,2,1,0:T(8,128)(2,1)} collective-permute-done((bf16[2,4,16,32,512]{4,3,2,1,0:T(8,128)(2,1)}, bf16[2,4,16,32,512]{4,3,2,1,0:T(8,128)(2,1)}, u32[]{:S(2)}, u32[]{:S(2)}) %collective-permute-start.4) | collective-permute-done | bytes 4194336 | tf_op jit(solution)/shard_map/ppermute | solution.py:21
  474.9 92.8 %collective-permute-done.5 = bf16[2,4,16,32,512]{4,3,2,1,0:T(8,128)(2,1)} collective-permute-done((bf16[2,4,16,32,512]{4,3,2,1,0:T(8,128)(2,1)}, bf16[2,4,16,32,512]{4,3,2,1,0:T(8,128)(2,1)}, u32[]{:S(2)}, u32[]{:S(2)}) %collective-permute-start.5) | collective-permute-done | bytes 4194336 | tf_op jit(solution)/shard_map/ppermute | solution.py:21
  578.9 12.1 %copy.96 = bf16[30,2,256,4,128]{4,3,2,1,0:T(4,128)(2,1)} copy(bf16[30,2,256,4,128]{4,2,3,1,0:T(8,128)(2,1)S(1)} %bitcast.240) | data formatting | bytes 31457280 | tf_op jit(solution)/shard_map/while | solution.py:159
  591.0 148.2 %while.22 = (s32[]{:T(128)}, bf16[3,2,256,4,128]{4,2,3,1,0:T(8,128)(2,1)S(1)}, s32[3,2,8]{2,1,0:T(2,128)S(1)}, bf16[30,2,256,4,128]{4,3,2,1,0:T(4,128)(2,1)}, pr...) while((s32[]{:T(128)}, bf16[3,2,256,4,128]{4,2,3,1,0:T(8,128)(2,1)S(1)}, ...), condition=%wide.region_3.10_spmd, body=%wide.region_0.9_spmd.sunk | while | flops 2177108992 | bytes 95458464 | solution.py:159
  591.1 14.4 %gather_fusion = bf16[16,2,256,4,128]{4,3,2,1,0:T(4,128)(2,1)} fusion(bf16[30,2,256,4,128]{4,3,2,1,0:T(4,128)(2,1)} %get-tuple-element.313, s32[1024]{0:T(1024)S(1)} %pad_clamp_fusion.2), kind=kCustom, calls=%fused_computation.clone.1 | custom fusion | bytes 16777280 | tf_op jit(solution)/shard_map/while/body/eval_jaxpr/jit(_take)/gather | solution.py:138
  619.6 10.2 %fusion.72 = (f32[2,4,256]{2,1,0:T(4,128)S(1)}, f32[2,4,256,2048]{3,2,1,0:T(8,128)}) fusion(pred[2,2048]{1,0:T(4,128)(4,1)S(1)} %bitcast.261, bf16[2,2048,4,128]{3,1,2,0:T(8,128)(2,1)} %bitcast.237, bf16[3,2,256,4,128]{4,2,3,1,0:T(8,128)(2,1)} %get-tuple-element.315, s32[]{:T(128)} %get-tuple-element.303), kind=kOutput, calls=%fused_computation.121.clone.1 | convolution fusion | flops 1090521088 | bytes 21508608 | tf_op jit(solution)/shard_map/while/body/eval_jaxpr/sub | solution.py:152
  629.9 10.1 %fusion.73 = bf16[1,2,256,4,128]{2,4,3,1,0:T(8,128)(2,1)S(1)} fusion(bf16[2,2048,4,128]{3,1,2,0:T(8,128)(2,1)} %bitcast.236, f32[2,4,256,2048]{3,2,1,0:T(8,128)} %get-tuple-element.294, f32[2,4,256]{2,1,0:T(4,128)S(1)} %get-tuple-element.295), kind=kOutput, calls=%fused_computation.12.clone.1 | convolution fusion | flops 1082392576 | bytes 21504000 | tf_op jit(solution)/shard_map/while/body/eval_jaxpr/phqk,pkhd->pqhd/dot_general | solution.py:154
  640.4 14.4 %gather_fusion = bf16[16,2,256,4,128]{4,3,2,1,0:T(4,128)(2,1)} fusion(bf16[30,2,256,4,128]{4,3,2,1,0:T(4,128)(2,1)} %get-tuple-element.313, s32[1024]{0:T(1024)S(1)} %pad_clamp_fusion.2), kind=kCustom, calls=%fused_computation.clone.1 | custom fusion | bytes 16777280 | tf_op jit(solution)/shard_map/while/body/eval_jaxpr/jit(_take)/gather | solution.py:138
  669.0 10.2 %fusion.72 = (f32[2,4,256]{2,1,0:T(4,128)S(1)}, f32[2,4,256,2048]{3,2,1,0:T(8,128)}) fusion(pred[2,2048]{1,0:T(4,128)(4,1)S(1)} %bitcast.261, bf16[2,2048,4,128]{3,1,2,0:T(8,128)(2,1)} %bitcast.237, bf16[3,2,256,4,128]{4,2,3,1,0:T(8,128)(2,1)} %get-tuple-element.315, s32[]{:T(128)} %get-tuple-element.303), kind=kOutput, calls=%fused_computation.121.clone.1 | convolution fusion | flops 1090521088 | bytes 21508608 | tf_op jit(solution)/shard_map/while/body/eval_jaxpr/sub | solution.py:152
  679.2 10.1 %fusion.73 = bf16[1,2,256,4,128]{2,4,3,1,0:T(8,128)(2,1)S(1)} fusion(bf16[2,2048,4,128]{3,1,2,0:T(8,128)(2,1)} %bitcast.236, f32[2,4,256,2048]{3,2,1,0:T(8,128)} %get-tuple-element.294, f32[2,4,256]{2,1,0:T(4,128)S(1)} %get-tuple-element.295), kind=kOutput, calls=%fused_computation.12.clone.1 | convolution fusion | flops 1082392576 | bytes 21504000 | tf_op jit(solution)/shard_map/while/body/eval_jaxpr/phqk,pkhd->pqhd/dot_general | solution.py:154
  689.8 14.4 %gather_fusion = bf16[16,2,256,4,128]{4,3,2,1,0:T(4,128)(2,1)} fusion(bf16[30,2,256,4,128]{4,3,2,1,0:T(4,128)(2,1)} %get-tuple-element.313, s32[1024]{0:T(1024)S(1)} %pad_clamp_fusion.2), kind=kCustom, calls=%fused_computation.clone.1 | custom fusion | bytes 16777280 | tf_op jit(solution)/shard_map/while/body/eval_jaxpr/jit(_take)/gather | solution.py:138
  718.3 10.2 %fusion.72 = (f32[2,4,256]{2,1,0:T(4,128)S(1)}, f32[2,4,256,2048]{3,2,1,0:T(8,128)}) fusion(pred[2,2048]{1,0:T(4,128)(4,1)S(1)} %bitcast.261, bf16[2,2048,4,128]{3,1,2,0:T(8,128)(2,1)} %bitcast.237, bf16[3,2,256,4,128]{4,2,3,1,0:T(8,128)(2,1)} %get-tuple-element.315, s32[]{:T(128)} %get-tuple-element.303), kind=kOutput, calls=%fused_computation.121.clone.1 | convolution fusion | flops 1090521088 | bytes 21508608 | tf_op jit(solution)/shard_map/while/body/eval_jaxpr/sub | solution.py:152
  728.5 10.1 %fusion.73 = bf16[1,2,256,4,128]{2,4,3,1,0:T(8,128)(2,1)S(1)} fusion(bf16[2,2048,4,128]{3,1,2,0:T(8,128)(2,1)} %bitcast.236, f32[2,4,256,2048]{3,2,1,0:T(8,128)} %get-tuple-element.294, f32[2,4,256]{2,1,0:T(4,128)S(1)} %get-tuple-element.295), kind=kOutput, calls=%fused_computation.12.clone.1 | convolution fusion | flops 1082392576 | bytes 21504000 | tf_op jit(solution)/shard_map/while/body/eval_jaxpr/phqk,pkhd->pqhd/dot_general | solution.py:154
  743.8 18.1 %collective-permute-done.7 = bf16[2,2,8,24,512]{4,3,2,0,1:T(8,128)(2,1)S(1)} collective-permute-done((bf16[2,2,8,24,512]{4,3,2,0,1:T(8,128)(2,1)S(1)}, bf16[2,2,8,24,512]{4,3,2,0,1:T(8,128)(2,1)S(1)}, u32[]{:S(2)}, u32[]{:S(2)}) %collective-permute-start.7) | collective-permute-done | bytes 786464 | tf_op jit(solution)/shard_map/ppermute | solution.py:15
  762.3 18.7 %collective-permute-done.8 = bf16[2,2,8,24,512]{4,3,2,1,0:T(8,128)(2,1)S(1)} collective-permute-done((bf16[2,2,8,24,512]{4,3,2,1,0:T(8,128)(2,1)S(1)}, bf16[2,2,8,24,512]{4,3,2,1,0:T(8,128)(2,1)S(1)}, u32[]{:S(2)}, u32[]{:S(2)}) %collective-permute-start.8) | collective-permute-done | bytes 786464 | tf_op jit(solution)/shard_map/ppermute | solution.py:15
  785.6 20.5 %all_to_all.33 = bf16[8,48,2048]{2,0,1:T(8,128)(2,1)S(1)} all-to-all(bf16[8,48,2048]{2,0,1:T(8,128)(2,1)S(1)} %copy.104), channel_id=1, replica_groups=mesh['slab'=16,'strip'=2] {'strip'}, dimensions={1} | all-to-all | bytes 3145728 | tf_op jit(solution)/shard_map/all_to_all | solution.py:174
  (110 shorter events, 140.6 us)
Async XLA Ops:
  73.7 60.4 %all-to-all-start = ((bf16[2,2,589824]{2,1,0:T(2,128)(2,1)}), bf16[2,2,589824]{2,1,0:T(2,128)(2,1)}, u32[]{:S(2)}, u32[]{:S(2)}) async-start(bf16[2,2,589824]{2,1,0:T(2,128)(2,1)} %reshape.576), calls=%async_computation | async-start | bytes 9437184 | tf_op jit(solution)/shard_map/all_to_all | solution.py:62
  220.7 2.1 copy-start
  222.8 4.7 collective-permute-start
  231.0 1.4 copy-start.2
  231.0 2.2 copy-start.3
  233.2 53.4 %collective-permute-start.1 = (bf16[2,2,3,8,24,512]{5,4,3,2,0,1:T(8,128)(2,1)S(1)}, bf16[2,2,3,8,24,512]{5,4,3,2,0,1:T(8,128)(2,1)}, u32[]{:S(2)}, u32[]{:S(2)}) collective-permute-start(bf16[2,2,3,8,24,512]{5,4,3,2,0,1:T(8,128)(2,1)S(1)} %broadcast_select_fusion.3), channel_id=1, source_target_pairs={{0,4},{2,6},{4,0},{6,2},{8,12},{10,14},{12,8},{14,10},{16,20},{18,... | collective-permute-start | bytes 7077896 | tf_op jit(solution)/shard_map/ppermute | solution.py:15
  290.9 2.1 copy-start.1
  293.0 52.8 %collective-permute-start.2 = (bf16[2,2,3,8,24,512]{5,4,3,2,1,0:T(8,128)(2,1)}, bf16[2,2,3,8,24,512]{5,4,3,2,1,0:T(8,128)(2,1)}, u32[]{:S(2)}, u32[]{:S(2)}) collective-permute-start(bf16[2,2,3,8,24,512]{5,4,3,2,1,0:T(8,128)(2,1)} %broadcast_select_fusion.5), channel_id=1, source_target_pairs={{0,8},{2,10},{4,12},{6,14},{8,0},{10,2},{12,4},{14,6},{16,24},{18,... | collective-permute-start | bytes 7077896 | tf_op jit(solution)/shard_map/ppermute | solution.py:15
  350.0 2.1 copy-start.4
  352.2 34.1 %copy-start.8 = (s32[8,3]{0,1:T(4,128)S(1)}, s32[8,3]{0,1:T(4,128)}, u32[]{:S(2)}) copy-start(s32[8,3]{0,1:T(4,128)} %param.33) | copy-start | bytes 292
  352.2 23.5 %collective-permute-start.3 = (bf16[2,4,16,8,512]{4,3,2,1,0:T(8,128)(2,1)S(1)}, bf16[2,4,16,8,512]{4,3,2,1,0:T(8,128)(2,1)S(1)}, u32[]{:S(2)}, u32[]{:S(2)}) collective-permute-start(bf16[2,4,16,8,512]{4,3,2,1,0:T(8,128)(2,1)S(1)} %slice_select_fusion), channel_id=1, source_target_pairs={{0,8},{2,10},{4,12},{6,14},{8,0},{10,2},{12,4},{14,6},{16,24},{18,... | collective-permute-start | bytes 3145736 | tf_op jit(solution)/shard_map/ppermute | solution.py:15
  375.8 2.7 copy-start.5
  378.4 92.5 %collective-permute-start.4 = (bf16[2,4,16,32,512]{4,3,2,1,0:T(8,128)(2,1)}, bf16[2,4,16,32,512]{4,3,2,1,0:T(8,128)(2,1)}, u32[]{:S(2)}, u32[]{:S(2)}) collective-permute-start(bf16[2,4,16,32,512]{4,3,2,1,0:T(8,128)(2,1)} %pad_maximum_fusion.5), channel_id=1, source_target_pairs={{0,16},{2,18},{4,20},{6,22},{8,24},{10,26},{12,28},{14,30},{1,17},... | collective-permute-start | bytes 12582920 | tf_op jit(solution)/shard_map/ppermute | solution.py:21
  385.0 182.6 %collective-permute-start.5 = (bf16[2,4,16,32,512]{4,3,2,1,0:T(8,128)(2,1)}, bf16[2,4,16,32,512]{4,3,2,1,0:T(8,128)(2,1)}, u32[]{:S(2)}, u32[]{:S(2)}) collective-permute-start(bf16[2,4,16,32,512]{4,3,2,1,0:T(8,128)(2,1)} %pad_maximum_fusion.5), channel_id=1, source_target_pairs={{16,0},{18,2},{20,4},{22,6},{24,8},{26,10},{28,12},{30,14},{17,1},... | collective-permute-start | bytes 12582920 | tf_op jit(solution)/shard_map/ppermute | solution.py:21
  386.6 3.4 copy-start.6
  578.9 12.1 %copy-start.7 = (bf16[3,2,256,4,128]{4,2,3,1,0:T(8,128)(2,1)S(1)}, bf16[3,2,256,4,128]{4,2,3,1,0:T(8,128)(2,1)}, u32[]{:S(2)}) copy-start(bf16[3,2,256,4,128]{4,2,3,1,0:T(8,128)(2,1)} %custom-call.2) | copy-start | bytes 4718596
  739.6 2.4 collective-permute-start.6
  742.3 19.6 %collective-permute-start.7 = (bf16[2,2,8,24,512]{4,3,2,0,1:T(8,128)(2,1)S(1)}, bf16[2,2,8,24,512]{4,3,2,0,1:T(8,128)(2,1)S(1)}, u32[]{:S(2)}, u32[]{:S(2)}) collective-permute-start(bf16[2,2,8,24,512]{4,3,2,0,1:T(8,128)(2,1)S(1)} %broadcast_select_fusion.15), channel_id=1, source_target_pairs={{0,4},{2,6},{4,0},{6,2},{8,12},{10,14},{12,8},{14,10},{16,20},{18,... | collective-permute-start | bytes 2359304 | tf_op jit(solution)/shard_map/ppermute | solution.py:15
  762.2 18.8 %collective-permute-start.8 = (bf16[2,2,8,24,512]{4,3,2,1,0:T(8,128)(2,1)S(1)}, bf16[2,2,8,24,512]{4,3,2,1,0:T(8,128)(2,1)S(1)}, u32[]{:S(2)}, u32[]{:S(2)}) collective-permute-start(bf16[2,2,8,24,512]{4,3,2,1,0:T(8,128)(2,1)S(1)} %broadcast_select_fusion.19), channel_id=1, source_target_pairs={{0,8},{2,10},{4,12},{6,14},{8,0},{10,2},{12,4},{14,6},{16,24},{18,... | collective-permute-start | bytes 2359304 | tf_op jit(solution)/shard_map/ppermute | solution.py:15
where the time goes:
time: 825 us; the launch traced here: 811 us
  waiting for transfers between devices  396 us (48%)
  local copies, waits for them, and re-layouts  257 us (31%)
  matrix products  60.9 us (7%)
  other arithmetic  54.6 us (7%)
  starting transfers between devices  20.6 us (2%)
  blocking collectives  20.5 us (2%)
    ppermute x2, waiting for transfers between devices, from_behind(): return lax.ppermute(block, axis, route)  173 us
    ppermute x7, waiting for transfers between devices, swapped(): return lax.ppermute(value, axis, pairs)  168 us
    unnamed x20, local copies, waits for them, and re-layouts  100 us
    all_to_all x1, waiting for transfers between devices, per_device(): lax.all_to_all(stacked, 'strip', split_axis=3, concat_axis=2, tiled=True)  54.5 us
    gather x3, local copies, waits for them, and re-layouts, attend(): window_tiles = jnp.take(key_tiles, tile_index.reshape(-1), axis=0)  43.3 us
    sub x3, matrix products, attend(): raised = jnp.exp((scores - row_max) * score_scale)  30.6 us
    dot_general x3, matrix products, attend(): jnp.einsum('phqk,pkhd->pqhd', weights, window_values, preferred_element_t...  30.2 us
    all_to_all x1, local copies, waits for them, and re-layouts, per_device(): lax.all_to_all(stacked, 'strip', split_axis=3, concat_axis=2, tiled=True)  25.3 us
  transfers between devices with their start and end apart: 10, of which 10 were waited for; matrix products, arithmetic and copies ran while one was open for 1% of the time, Pallas kernels for 0%

commit v1 on v0

--- a/solution.py
+++ b/solution.py
@@ -1,6 +1,11 @@
+import functools
+import math
+
 import jax
 import jax.numpy as jnp
 from jax import lax
+from jax.experimental import pallas as pl
+from jax.experimental.pallas import tpu as pltpu
 from jax.sharding import PartitionSpec as P
 
 HD = 128
@@ -174,16 +179,234 @@
     return lax.all_to_all(merged, "strip", split_axis=1, concat_axis=2, tiled=True)
 
 
+BY = 4
+FT = TILE_T
+COLS = 3
+ROW_TILES = 2
+COL_TILES = 6
+TOKENS = TILE_T * TILE_H * TILE_W
+
+
+def head_kernel(layers, windows, off_ref, q_ref, k_ref, v_ref, out_ref, kv_in, q_in, o_buf,
+                k_tiles, v_tiles, q_wide, o_wide, kv_sems, q_sems, out_sem, kv_sent, q_sent,
+                o_sent):
+    devices = layers * FT * BY
+    tiles = layers * ROW_TILES * COL_TILES
+    me = lax.axis_index("slab") * 2 + lax.axis_index("strip")
+    layer, frame, lane = me // (FT * BY), me // BY % FT, me % BY
+
+    def mesh_id(device):
+        return (device // 2, device % 2)
+
+    def device_of(a, f, b):
+        return (a * FT + f) * BY + b
+
+    def columns(device):
+        return pl.ds(pl.multiple_of(device * HD, HD), HD)
+
+    barrier = pltpu.get_barrier_semaphore()
+
+    @pl.loop(1, devices)
+    def _(i):
+        pl.semaphore_signal(
+            barrier, inc=1, device_id=mesh_id((me + i) % devices),
+            device_id_type=pl.DeviceIdType.MESH,
+        )
+
+    pl.semaphore_wait(barrier, devices - 1)
+
+    def kv_step(i):
+        return (layers - 1) - i % layers, i // layers % FT, i // (layers * FT)
+
+    def q_step(i):
+        return (layers - 1) - i // FT % layers, i % FT, i // (layers * FT)
+
+    def ahead(step):
+        a, f, b = step
+        return device_of((layer + a) % layers, (frame + f) % FT, (lane + b) % BY)
+
+    kv_self = layers - 1
+    q_self = (layers - 1) * FT
+    my_group = layer * BY + lane
+
+    pltpu.make_async_copy(k_ref.at[:, columns(me)], kv_in.at[me, 0], kv_sems.at[me]).start()
+    pltpu.make_async_copy(v_ref.at[:, columns(me)], kv_in.at[me, 1], kv_sems.at[me]).start()
+    pltpu.make_async_copy(
+        q_ref.at[:, columns(me)], q_in.at[my_group, frame], q_sems.at[my_group]
+    ).start()
+
+    def send_kv(i):
+        to = ahead(kv_step(i))
+        for part, ref in enumerate((k_ref, v_ref)):
+            pltpu.make_async_remote_copy(
+                src_ref=ref.at[:, columns(to)],
+                dst_ref=kv_in.at[me, part],
+                send_sem=kv_sent,
+                recv_sem=kv_sems.at[me],
+                device_id=mesh_id(to),
+                device_id_type=pl.DeviceIdType.MESH,
+            ).start()
+
+    def send_q(i):
+        to = ahead(q_step(i))
+        pltpu.make_async_remote_copy(
+            src_ref=q_ref.at[:, columns(to)],
+            dst_ref=q_in.at[my_group, frame],
+            send_sem=q_sent,
+            recv_sem=q_sems.at[my_group],
+            device_id=mesh_id(to),
+            device_id_type=pl.DeviceIdType.MESH,
+        ).start()
+
+    for send, own in ((send_kv, kv_self), (send_q, q_self)):
+        pl.loop(0, own)(send)
+        pl.loop(own + 1, devices)(send)
+
+    @pl.loop(0, tiles)
+    def _(t):
+        v_tiles[t, :, :, HD:] = jnp.ones((FT, 64, HD), jnp.bfloat16)
+
+    v_tiles[tiles] = jnp.zeros((FT, 64, 2 * HD), jnp.bfloat16)
+
+    @pl.loop(0, devices)
+    def _(i):
+        a, f, b = kv_step(i)
+        a, f, b = (layer + layers - a) % layers, (frame + FT - f) % FT, (lane + BY - b) % BY
+        source = device_of(a, f, b)
+        pltpu.make_async_copy(kv_in.at[source], kv_in.at[source], kv_sems.at[source]).wait()
+        first = (a * ROW_TILES + b // 2) * COL_TILES + b % 2 * COLS
+        key_block = kv_in[source, 0].astype(jnp.float32).reshape(TILE_H, COLS, TILE_W, HD)
+        value_block = kv_in[source, 1].astype(jnp.float32).reshape(TILE_H, COLS, TILE_W, HD)
+        for c in range(COLS):
+            k_tiles[first + c, f] = key_block[:, c].reshape(64, HD).astype(jnp.bfloat16)
+            v_tiles[first + c, f, :, :HD] = (
+                value_block[:, c].reshape(64, HD).astype(jnp.bfloat16)
+            )
+
+    factor = HD ** (-0.5) * math.log2(math.e)
+
+    @pl.loop(0, layers * BY)
+    def _(n):
+        a = (layer + layers - ((layers - 1) - n % layers)) % layers
+        b = (lane + BY - n // layers) % BY
+        group = a * BY + b
+        pltpu.make_async_copy(q_in.at[group], q_in.at[group], q_sems.at[group]).wait()
+        q_wide[...] = q_in[group].astype(jnp.float32).reshape(FT, TILE_H, COLS, TILE_W, HD)
+
+        @pl.loop(0, COLS)
+        def _(c):
+            row, col = b // 2, b % 2 * COLS + c
+            own = (a * ROW_TILES + row) * COL_TILES + col
+            query = q_wide[:, :, c].reshape(TOKENS, HD).astype(jnp.bfloat16)
+            scores, picks = [], []
+            for w in range(windows):
+                ka, kr, kc = a + off_ref[w, 0], row + off_ref[w, 1], col + off_ref[w, 2]
+                live = (ka >= 0) & (ka < layers) & (kr >= 0) & (kr < ROW_TILES)
+                live = live & (kc >= 0) & (kc < COL_TILES)
+                tile = (ka * ROW_TILES + kr) * COL_TILES + kc
+                picks.append(jnp.where(live, tile, tiles))
+                keys = k_tiles[jnp.where(live, tile, own)].reshape(TOKENS, HD)
+                scores.append(
+                    lax.dot_general(
+                        query, keys, (((1,), (1,)), ((), ())),
+                        preferred_element_type=jnp.float32,
+                    )
+                )
+            top = functools.reduce(jnp.maximum, scores)
+            top = jnp.max(top, axis=-1, keepdims=True)
+            total = jnp.zeros((TOKENS, 2 * HD), jnp.float32)
+            for score, pick in zip(scores, picks):
+                raised = jnp.exp2((score - top) * factor).astype(jnp.bfloat16)
+                values = v_tiles[pick].reshape(TOKENS, 2 * HD)
+                total += jnp.dot(raised, values, preferred_element_type=jnp.float32)
+            mixed = total[:, :HD] / total[:, HD:]
+            o_wide[:, :, c] = mixed.reshape(FT, TILE_H, TILE_W, HD)
+
+        o_buf[group] = o_wide[...].reshape(FT, 192, HD).astype(jnp.bfloat16)
+
+        @pl.loop(0, FT)
+        def _(f):
+            to = device_of(a, f, b)
+
+            @pl.when(to == me)
+            def _():
+                pltpu.make_async_copy(
+                    o_buf.at[group, f], out_ref.at[:, columns(me)], out_sem
+                ).start()
+
+            @pl.when(to != me)
+            def _():
+                pltpu.make_async_remote_copy(
+                    src_ref=o_buf.at[group, f],
+                    dst_ref=out_ref.at[:, columns(me)],
+                    send_sem=o_sent,
+                    recv_sem=out_sem,
+                    device_id=mesh_id(to),
+                    device_id_type=pl.DeviceIdType.MESH,
+                ).start()
+
+    others = pl.ds(0, devices - 1)
+    pltpu.make_async_copy(kv_in.at[others], kv_in.at[others], kv_sent).wait()
+    sent = kv_in.at[others, 0]
+    pltpu.make_async_copy(sent, sent, q_sent).wait()
+    pltpu.make_async_copy(sent, sent, o_sent).wait()
+    pltpu.make_async_copy(out_ref, out_ref, out_sem).wait()
+
+
+def by_head(query_rows, key_rows, value_rows, window_offsets):
+    shape = query_rows.shape
+    devices = lax.axis_size("slab") * lax.axis_size("strip")
+    layers = devices // (FT * BY)
+    tiles = layers * ROW_TILES * COL_TILES
+    windows = window_offsets.shape[0]
+    tokens, width = shape[0] * shape[1], shape[2]
+    flat = [x.reshape(tokens, width) for x in (query_rows, key_rows, value_rows)]
+    pairs = tiles * windows * TOKENS * TOKENS
+    out = pl.pallas_call(
+        functools.partial(head_kernel, layers, windows),
+        out_shape=jax.ShapeDtypeStruct((tokens, width), jnp.bfloat16),
+        in_specs=[pl.BlockSpec(memory_space=pltpu.SMEM)]
+        + [pl.BlockSpec(memory_space=pl.ANY)] * 3,
+        out_specs=pl.BlockSpec(memory_space=pl.ANY),
+        scratch_shapes=[
+            pltpu.VMEM((devices, 2, tokens, HD), jnp.bfloat16),
+            pltpu.VMEM((layers * BY, FT, tokens, HD), jnp.bfloat16),
+            pltpu.VMEM((layers * BY, FT, tokens, HD), jnp.bfloat16),
+            pltpu.VMEM((tiles, FT, 64, HD), jnp.bfloat16),
+            pltpu.VMEM((tiles + 1, FT, 64, 2 * HD), jnp.bfloat16),
+            pltpu.VMEM((FT, TILE_H, COLS, TILE_W, HD), jnp.float32),
+            pltpu.VMEM((FT, TILE_H, COLS, TILE_W, HD), jnp.float32),
+            pltpu.SemaphoreType.DMA((devices,)),
+            pltpu.SemaphoreType.DMA((layers * BY,)),
+            pltpu.SemaphoreType.DMA,
+            pltpu.SemaphoreType.DMA,
+            pltpu.SemaphoreType.DMA,
+            pltpu.SemaphoreType.DMA,
+        ],
+        compiler_params=pltpu.CompilerParams(
+            collective_id=0, has_side_effects=True, vmem_limit_bytes=40 * 2**20
+        ),
+        cost_estimate=pl.CostEstimate(
+            flops=6 * pairs * HD, bytes_accessed=8 * tokens * width, transcendentals=pairs
+        ),
+    )(window_offsets, *flat)
+    return out.reshape(shape)
+
+
 def solution(mesh):
-    return jax.shard_map(
-        per_device,
-        mesh=mesh,
-        in_specs=(
-            P("slab", "strip", None),
-            P("slab", "strip", None),
-            P("slab", "strip", None),
-            P(),
-        ),
-        out_specs=P("slab", "strip", None),
-        check_vma=False,
-    )
+    specs = P("slab", "strip", None)
+
+    def attention(query_rows, key_rows, value_rows, window_offsets):
+        slabs, strips = mesh.shape["slab"], mesh.shape["strip"]
+        lines, width, features = query_rows.shape
+        fits = slabs * strips * HD == features and lines == slabs * TILE_H
+        fits = fits and strips == 2 and width == strips * COLS * TILE_W and slabs % 8 == 0
+        return jax.shard_map(
+            by_head if fits else per_device,
+            mesh=mesh,
+            in_specs=(specs, specs, specs, P()),
+            out_specs=specs,
+            check_vma=False,
+        )(query_rows, key_rows, value_rows, window_offsets)
+
+    return attention

time: 825 us -> 151 us (0.18); the launches traced: 811 us -> 150 us
  waiting for transfers between devices: 396 us -> 0 us
  local copies, waits for them, and re-layouts: 257 us -> 6.12 us
  Pallas kernels: 0 us -> 144 us
  matrix products: 60.9 us -> 0 us
  other arithmetic: 54.6 us -> 0 us
  starting transfers between devices: 20.6 us -> 0 us
  blocking collectives: 20.5 us -> 0 us
    ppermute x9 -> x0, waiting for transfers between devices: 341 us -> none  [the longest x2 173 us: from_behind(): return lax.ppermute(block, axis, route)]
    pallas_call x0 -> x1, Pallas kernels: none -> 144 us  [by_head(): pl.pallas_call(functools.partial(head_kernel, layers, windows), out_shape...]
    unnamed x20 -> x8, local copies, waits for them, and re-layouts: 100 us -> 6.12 us
    all_to_all x1 -> x0, waiting for transfers between devices: 54.5 us -> none  [per_device(): lax.all_to_all(stacked, 'strip', split_axis=3, concat_axis=2, tiled=True)]
    gather x3 -> x0, local copies, waits for them, and re-layouts: 43.3 us -> none  [attend(): window_tiles = jnp.take(key_tiles, tile_index.reshape(-1), axis=0)]
    sub x3 -> x0, matrix products: 30.6 us -> none  [attend(): raised = jnp.exp((scores - row_max) * score_scale)]
    select_n x18 -> x0, other arithmetic: 30.4 us -> none  [the longest x6 24.4 us: attend(): window_tiles = jnp.take(key_tiles, tile_index.reshape(-1), axis=0)]
    dot_general x3 -> x0, matrix products: 30.2 us -> none  [attend(): jnp.einsum('phqk,pkhd->pqhd', weights, window_values, preferred_element_t...]
  transfers between devices with their start and end apart: 10 -> 0, of which waited for: 10 -> 0; matrix products, arithmetic and copies ran while one was open for 1% -> 0% of each run, Pallas kernels for 0% -> 0%
where the time goes in v1:
time: 151 us; the launch traced here: 150 us
  Pallas kernels  144 us (95%)
  local copies, waits for them, and re-layouts  6.12 us (4%)
    pallas_call x1, Pallas kernels, by_head(): pl.pallas_call(functools.partial(head_kernel, layers, windows), out_shape...  144 us
    unnamed x8, local copies, waits for them, and re-layouts  6.12 us

profile of v1, /device:TPU:0, one launch (start us, length us, event | category | flops | bytes accessed | tf_op | source)
XLA Modules:
  0.0 149.8 jit_solution(16059058931728077749)
XLA Ops:
  0.0 0.8 copy.5.off_ref
  0.8 0.0 copy-start
  0.8 1.4 copy-done
  2.2 0.0 copy-start.1
  2.2 1.4 copy-done.1
  3.6 0.0 copy-start.2
  3.6 1.4 copy-done.2
  5.0 143.7 %shard_map.46 = bf16[192,4096]{1,0:T(8,128)(2,1)S(1)} custom-call(s32[8,3]{1,0:T(8,128)S(1)} %copy.5.off_ref, bf16[192,4096]{1,0:T(8,128)(2,1)S(1)} %bitcast.5, bf16[192,4096]{1,0:T(8,128)(2,1)S(1)} %bitcast.6, bf16[192,4096]{1,0:T(8,128)(2,1)S(1)} %bitcast.7), custom_call_target="tpu_custom_call" | custom-call | flops 9663676416 | bytes 6291456 | tf_op jit(solution)/shard_map/pallas_call | solution.py:365
  148.7 1.1 copy.7
Async XLA Ops:
  0.8 1.4 copy-start
  2.2 1.4 copy-start.1
  3.6 1.4 copy-start.2

commit v2 on v1

--- a/solution.py
+++ b/solution.py
@@ -218,15 +218,20 @@
     def kv_step(i):
         return (layers - 1) - i % layers, i // layers % FT, i // (layers * FT)
 
+    def group_step(n):
+        return (layers - 1) - n // 2 % layers, n // (2 * layers) * 2 + n % 2
+
     def q_step(i):
-        return (layers - 1) - i // FT % layers, i % FT, i // (layers * FT)
+        a, b = group_step(i // FT)
+        return a, i % FT, b
 
     def ahead(step):
         a, f, b = step
         return device_of((layer + a) % layers, (frame + f) % FT, (lane + b) % BY)
 
     kv_self = layers - 1
-    q_self = (layers - 1) * FT
+    q_self = (layers - 1) * 2 * FT
+    q_early = devices // 2
     my_group = layer * BY + lane
 
     pltpu.make_async_copy(k_ref.at[:, columns(me)], kv_in.at[me, 0], kv_sems.at[me]).start()
@@ -258,9 +263,10 @@
             device_id_type=pl.DeviceIdType.MESH,
         ).start()
 
-    for send, own in ((send_kv, kv_self), (send_q, q_self)):
-        pl.loop(0, own)(send)
-        pl.loop(own + 1, devices)(send)
+    pl.loop(0, kv_self)(send_kv)
+    pl.loop(kv_self + 1, devices)(send_kv)
+    pl.loop(0, q_self)(send_q)
+    pl.loop(q_self + 1, q_early)(send_q)
 
     @pl.loop(0, tiles)
     def _(t):
@@ -270,6 +276,10 @@
 
     @pl.loop(0, devices)
     def _(i):
+        @pl.when(i >= q_early)
+        def _():
+            send_q(i)
+
         a, f, b = kv_step(i)
         a, f, b = (layer + layers - a) % layers, (frame + FT - f) % FT, (lane + BY - b) % BY
         source = device_of(a, f, b)
@@ -287,8 +297,8 @@
 
     @pl.loop(0, layers * BY)
     def _(n):
-        a = (layer + layers - ((layers - 1) - n % layers)) % layers
-        b = (lane + BY - n // layers) % BY
+        a, b = group_step(n)
+        a, b = (layer + layers - a) % layers, (lane + BY - b) % BY
         group = a * BY + b
         pltpu.make_async_copy(q_in.at[group], q_in.at[group], q_sems.at[group]).wait()
         q_wide[...] = q_in[group].astype(jnp.float32).reshape(FT, TILE_H, COLS, TILE_W, HD)
@@ -300,7 +310,7 @@
             query = q_wide[:, :, c].reshape(TOKENS, HD).astype(jnp.bfloat16)
             scores, picks = [], []
             for w in range(windows):
-                ka, kr, kc = a + off_ref[w, 0], row + off_ref[w, 1], col + off_ref[w, 2]
+                ka, kr, kc = a + off_ref[0, w], row + off_ref[1, w], col + off_ref[2, w]
                 live = (ka >= 0) & (ka < layers) & (kr >= 0) & (kr < ROW_TILES)
                 live = live & (kc >= 0) & (kc < COL_TILES)
                 tile = (ka * ROW_TILES + kr) * COL_TILES + kc
@@ -384,12 +394,12 @@
             pltpu.SemaphoreType.DMA,
         ],
         compiler_params=pltpu.CompilerParams(
-            collective_id=0, has_side_effects=True, vmem_limit_bytes=40 * 2**20
+            collective_id=0, has_side_effects=True, vmem_limit_bytes=60 * 2**20
         ),
         cost_estimate=pl.CostEstimate(
             flops=6 * pairs * HD, bytes_accessed=8 * tokens * width, transcendentals=pairs
         ),
-    )(window_offsets, *flat)
+    )(window_offsets.T, *flat)
     return out.reshape(shape)
 
 

time: 151 us -> 147 us (0.974)
  local copies, waits for them, and re-layouts: 6.12 us -> 2.7 us
    unnamed x8 -> x1, local copies, waits for them, and re-layouts: 6.12 us -> 2.7 us
where the time goes in v2:
time: 147 us; the launch traced here: 146 us
  Pallas kernels  144 us (98%)
  local copies, waits for them, and re-layouts  2.7 us (2%)
    pallas_call x1, Pallas kernels, by_head(): pl.pallas_call(functools.partial(head_kernel, layers, windows), out_shape...  144 us

profile of v2, /device:TPU:0, one launch (start us, length us, event | category | flops | bytes accessed | tf_op | source)
XLA Modules:
  0.0 146.5 jit_solution(12583302785827123374)
XLA Ops:
  0.0 143.8 %shard_map.46 = bf16[192,4096]{1,0:T(8,128)(2,1)} custom-call(s32[3,8]{1,0:T(4,128)} %bitcast.9, bf16[192,4096]{1,0:T(8,128)(2,1)} %bitcast.6, bf16[192,4096]{1,0:T(8,128)(2,1)} %bitcast.7, bf16[192,4096]{1,0:T(8,128)(2,1)} %bitcast.8), custom_call_target="tpu_custom_call" | custom-call | flops 9663676416 | bytes 6291456 | tf_op jit(solution)/shard_map/pallas_call | solution.py:375
  143.8 2.7 %copy.6 = bf16[8,24,4096]{2,1,0:T(8,128)(2,1)} copy(bf16[8,24,4096]{2,1,0:T(8,128)(2,1)} %bitcast.5) | data formatting | bytes 3145728

commit v3 on v2

--- a/solution.py
+++ b/solution.py
@@ -374,7 +374,7 @@
     pairs = tiles * windows * TOKENS * TOKENS
     out = pl.pallas_call(
         functools.partial(head_kernel, layers, windows),
-        out_shape=jax.ShapeDtypeStruct((tokens, width), jnp.bfloat16),
+        out_shape=pltpu.VMEM((tokens, width), jnp.bfloat16),
         in_specs=[pl.BlockSpec(memory_space=pltpu.SMEM)]
         + [pl.BlockSpec(memory_space=pl.ANY)] * 3,
         out_specs=pl.BlockSpec(memory_space=pl.ANY),

time: 147 us -> 146 us (level)
  local copies, waits for them, and re-layouts: 2.7 us -> 1.15 us
    unnamed x1, local copies, waits for them, and re-layouts: 2.7 us -> 1.15 us
where the time goes in v3:
time: 146 us; the launch traced here: 145 us
  Pallas kernels  144 us (99%)
    pallas_call x1, Pallas kernels, by_head(): pl.pallas_call(functools.partial(head_kernel, layers, windows), out_shape...  144 us

profile of v3, /device:TPU:0, one launch (start us, length us, event | category | flops | bytes accessed | tf_op | source)
XLA Modules:
  0.0 144.9 jit_solution(1784812718978837869)
XLA Ops:
  0.0 143.7 %shard_map.46 = bf16[192,4096]{1,0:T(8,128)(2,1)S(1)} custom-call(s32[3,8]{1,0:T(4,128)} %bitcast.9, bf16[192,4096]{1,0:T(8,128)(2,1)} %bitcast.6, bf16[192,4096]{1,0:T(8,128)(2,1)} %bitcast.7, bf16[192,4096]{1,0:T(8,128)(2,1)} %bitcast.8), custom_call_target="tpu_custom_call" | custom-call | flops 9663676416 | bytes 6291456 | tf_op jit(solution)/shard_map/pallas_call | solution.py:375
  143.7 1.1 copy.6

commit v4 on v3

--- a/solution.py
+++ b/solution.py
@@ -196,7 +196,7 @@
     layer, frame, lane = me // (FT * BY), me // BY % FT, me % BY
 
     def mesh_id(device):
-        return (device // 2, device % 2)
+        return (lax.div(device, 2), lax.rem(device, 2))
 
     def device_of(a, f, b):
         return (a * FT + f) * BY + b
@@ -209,29 +209,10 @@
     @pl.loop(1, devices)
     def _(i):
         pl.semaphore_signal(
-            barrier, inc=1, device_id=mesh_id((me + i) % devices),
+            barrier, inc=1, device_id=mesh_id(lax.rem(me + i, devices)),
             device_id_type=pl.DeviceIdType.MESH,
         )
 
-    pl.semaphore_wait(barrier, devices - 1)
-
-    def kv_step(i):
-        return (layers - 1) - i % layers, i // layers % FT, i // (layers * FT)
-
-    def group_step(n):
-        return (layers - 1) - n // 2 % layers, n // (2 * layers) * 2 + n % 2
-
-    def q_step(i):
-        a, b = group_step(i // FT)
-        return a, i % FT, b
-
-    def ahead(step):
-        a, f, b = step
-        return device_of((layer + a) % layers, (frame + f) % FT, (lane + b) % BY)
-
-    kv_self = layers - 1
-    q_self = (layers - 1) * 2 * FT
-    q_early = devices // 2
     my_group = layer * BY + lane
 
     pltpu.make_async_copy(k_ref.at[:, columns(me)], kv_in.at[me, 0], kv_sems.at[me]).start()
@@ -240,6 +221,31 @@
         q_ref.at[:, columns(me)], q_in.at[my_group, frame], q_sems.at[my_group]
     ).start()
 
+    @pl.loop(0, tiles)
+    def _(t):
+        v_tiles[t, :, :, HD:] = jnp.ones((FT, 64, HD), jnp.bfloat16)
+
+    v_tiles[tiles] = jnp.zeros((FT, 64, 2 * HD), jnp.bfloat16)
+
+    pl.semaphore_wait(barrier, devices - 1)
+
+    def kv_step(i):
+        return (layers - 1) - i % layers, i // layers % FT, i // (layers * FT)
+
+    def group_step(n):
+        return (layers - 1) - n // 2 % layers, n // (2 * layers) * 2 + n % 2
+
+    def q_step(i):
+        a, b = group_step(i // FT)
+        return a, i % FT, b
+
+    def ahead(step):
+        a, f, b = step
+        return device_of((layer + a) % layers, (frame + f) % FT, (lane + b) % BY)
+
+    kv_self = layers - 1
+    q_self = (layers - 1) * 2 * FT
+    q_early = devices // 2
     def send_kv(i):
         to = ahead(kv_step(i))
         for part, ref in enumerate((k_ref, v_ref)):
@@ -267,12 +273,6 @@
     pl.loop(kv_self + 1, devices)(send_kv)
     pl.loop(0, q_self)(send_q)
     pl.loop(q_self + 1, q_early)(send_q)
-
-    @pl.loop(0, tiles)
-    def _(t):
-        v_tiles[t, :, :, HD:] = jnp.ones((FT, 64, HD), jnp.bfloat16)
-
-    v_tiles[tiles] = jnp.zeros((FT, 64, 2 * HD), jnp.bfloat16)
 
     @pl.loop(0, devices)
     def _(i):
@@ -335,7 +335,8 @@
         o_buf[group] = o_wide[...].reshape(FT, 192, HD).astype(jnp.bfloat16)
 
         @pl.loop(0, FT)
-        def _(f):
+        def _(turn):
+            f = lax.rem(frame + turn, FT)
             to = device_of(a, f, b)
 
             @pl.when(to == me)

time: 146 us -> 147 us (level)
    pallas_call x1, Pallas kernels: 144 us -> 145 us  [by_head(): pl.pallas_call(functools.partial(head_kernel, layers, windows), out_shape...]
where the time goes in v4:
time: 147 us
  Pallas kernels  145 us (99%)
    pallas_call x1, Pallas kernels, by_head(): pl.pallas_call(functools.partial(head_kernel, layers, windows), out_shape...  145 us

profile of v4, /device:TPU:0, one launch (start us, length us, event | category | flops | bytes accessed | tf_op | source)
XLA Modules:
  0.0 146.6 jit_solution(17108396290202578750)
XLA Ops:
  0.0 145.4 %shard_map.46 = bf16[192,4096]{1,0:T(8,128)(2,1)S(1)} custom-call(s32[3,8]{1,0:T(4,128)} %bitcast.9, bf16[192,4096]{1,0:T(8,128)(2,1)} %bitcast.6, bf16[192,4096]{1,0:T(8,128)(2,1)} %bitcast.7, bf16[192,4096]{1,0:T(8,128)(2,1)} %bitcast.8), custom_call_target="tpu_custom_call" | custom-call | flops 9663676416 | bytes 6291456 | tf_op jit(solution)/shard_map/pallas_call | solution.py:376
  145.5 1.1 copy.6

commit v5 on v3

--- a/solution.py
+++ b/solution.py
@@ -216,7 +216,7 @@
     pl.semaphore_wait(barrier, devices - 1)
 
     def kv_step(i):
-        return (layers - 1) - i % layers, i // layers % FT, i // (layers * FT)
+        return (layers - 1) - i // (FT * BY), i % FT, i // FT % BY
 
     def group_step(n):
         return (layers - 1) - n // 2 % layers, n // (2 * layers) * 2 + n % 2
@@ -229,7 +229,8 @@
         a, f, b = step
         return device_of((layer + a) % layers, (frame + f) % FT, (lane + b) % BY)
 
-    kv_self = layers - 1
+    kv_self = (layers - 1) * FT * BY
+    lead = FT * BY // 2
     q_self = (layers - 1) * 2 * FT
     q_early = devices // 2
     my_group = layer * BY + lane
@@ -263,10 +264,17 @@
             device_id_type=pl.DeviceIdType.MESH,
         ).start()
 
-    pl.loop(0, kv_self)(send_kv)
-    pl.loop(kv_self + 1, devices)(send_kv)
-    pl.loop(0, q_self)(send_q)
-    pl.loop(q_self + 1, q_early)(send_q)
+    @pl.loop(0, kv_self + lead)
+    def _(j):
+        pl.when(j < kv_self)(lambda: send_kv(j))
+        near = kv_self + j - (kv_self + lead - FT * BY)
+        pl.when(near > kv_self)(lambda: send_kv(near))
+
+        @pl.when(j >= kv_self)
+        def _():
+            for k in range(q_early // lead):
+                query = (j - kv_self) * (q_early // lead) + k
+                pl.when(query != q_self)(lambda query=query: send_q(query))
 
     @pl.loop(0, tiles)
     def _(t):
@@ -276,9 +284,9 @@
 
     @pl.loop(0, devices)
     def _(i):
-        @pl.when(i >= q_early)
+        @pl.when((i >= lead) & (i < lead + devices - q_early))
         def _():
-            send_q(i)
+            send_q(i - lead + q_early)
 
         a, f, b = kv_step(i)
         a, f, b = (layer + layers - a) % layers, (frame + FT - f) % FT, (lane + BY - b) % BY

time: 146 us -> 147 us (level)
  no operation moved by 1% of the time
where the time goes in v5:
time: 147 us; the launch traced here: 146 us
  Pallas kernels  145 us (99%)
    pallas_call x1, Pallas kernels, by_head(): pl.pallas_call(functools.partial(head_kernel, layers, windows), out_shape...  145 us

profile of v5, /device:TPU:0, one launch (start us, length us, event | category | flops | bytes accessed | tf_op | source)
XLA Modules:
  0.0 146.1 jit_solution(12202729580445538111)
XLA Ops:
  0.0 144.9 %shard_map.46 = bf16[192,4096]{1,0:T(8,128)(2,1)S(1)} custom-call(s32[3,8]{1,0:T(4,128)} %bitcast.9, bf16[192,4096]{1,0:T(8,128)(2,1)} %bitcast.6, bf16[192,4096]{1,0:T(8,128)(2,1)} %bitcast.7, bf16[192,4096]{1,0:T(8,128)(2,1)} %bitcast.8), custom_call_target="tpu_custom_call" | custom-call | flops 9663676416 | bytes 6291456 | tf_op jit(solution)/shard_map/pallas_call | solution.py:383
  144.9 1.1 copy.6
